TPU v7x, 256 devices: a whole 4x4x8 slice. The times are simulated.
256 devices in a mesh: seq: 32 (over y, x, core), head: 8 (over z).
Axes of the slice: x: 4, y: 4, z: 8, core: 2. Of those that a mesh axis runs over, the one named last changes fastest.
Arguments:
- q_values: bfloat16 [65536, 4096], P('seq', 'head'), may hold values from -6 to 6
- k_values: bfloat16 [65536, 4096], P('seq', 'head'), may hold values from -6 to 6
- v_values: bfloat16 [65536, 4096], P('seq', 'head'), may hold values from -6 to 6
- q_scales: float32 [65536, 32], P('seq', 'head'), may hold values from 0.5 to 4
- k_scales: float32 [65536, 32], P('seq', 'head'), may hold values from 0.5 to 4
- v_scales: float32 [65536, 32], P('seq', 'head'), may hold values from 0.5 to 2
- conv_weight: float32 [32, 33], P('head'), may hold values from -0.9 to 0.9
Outputs:
- attended: bfloat16 [65536, 4096], P('seq', 'head')
All inputs are finite; a program needn't handle non-finite values.
Results may differ from a plain program's by a relative error of at most 0.03.
Values may be sent and summed in bfloat16 or wider, within the bound.
A program may use at most 128 MiB of HBM per device.

v0:
```python
import functools
import jax
import jax.numpy as jnp
from jax import lax
from jax.sharding import Mesh
from jax.sharding import PartitionSpec as P

HEAD_DIM = 128
LANDMARKS = 256
SWEEPS = 6
SEQ = ("seq_0", "seq_1", "seq_2")


def side_by_side(arrays, axis, dim, along):
    both = jnp.concatenate(arrays, axis=along)
    result, at, finished = (lax.all_gather(both, axis, axis=dim, tiled=True), 0, [])
    for a in arrays:
        finished.append(lax.slice_in_dim(result, at, at + a.shape[along], axis=along))
        at += a.shape[along]
    return tuple(finished)


def from_everyone(shard, axis):
    copies = jnp.broadcast_to(shard, (lax.axis_size(axis), *shard.shape))
    return lax.all_to_all(copies, axis, split_axis=0, concat_axis=0, tiled=True)


def taken_together(shard, axis):
    everything = from_everyone(shard, axis)
    return jnp.max(everything, axis=0)


def packed_total(arrays, axis):
    line, at, finished = (jnp.concatenate([a.reshape(-1) for a in arrays]), 0, [])
    total = taken_together(line, axis)
    for a in arrays:
        finished.append(total[at : at + a.size].reshape(a.shape))
        at += a.size
    return tuple(finished)


def by_axis(shard, axes):
    return functools.reduce(lax.pmax, axes, shard)


def padded_2(shard, sides, width):
    for axis, dim in sides:
        count, length = (lax.axis_size(axis), shard.shape[dim])
        up = [(i, (i + 1) % count) for i in range(count - 1)]
        down = [(j, i) for i, j in up]
        last = lax.slice_in_dim(shard, length - width, length, axis=dim)
        leading = lax.slice_in_dim(shard, 0, width, axis=dim)
        before = lax.ppermute(last, axis, up)
        after = lax.ppermute(leading, axis, down)
        shard = jnp.concatenate([before, shard, after], axis=dim)
    return shard


def dequant(value_rows, scales):
    count = scales.shape[1]
    shaped = value_rows.reshape(value_rows.shape[0], count, HEAD_DIM).astype(jnp.float32)
    return (shaped * scales[:, :, None]).astype(jnp.bfloat16)


def newton(kernel, initial, right_side):
    eye_matrix = jnp.eye(kernel.shape[0], dtype=jnp.float32)
    iterate = initial
    for sweep in range(SWEEPS):
        product = jnp.dot(kernel, iterate)
        inner_term = 7.0 * eye_matrix - product
        inner_term = 15.0 * eye_matrix - jnp.dot(product, inner_term)
        inner_term = 13.0 * eye_matrix - jnp.dot(product, inner_term)
        iterate = 0.25 * jnp.dot(iterate, inner_term)
    return jnp.dot(iterate, right_side).astype(jnp.bfloat16)


def shards(q_values, k_values, v_values, q_scales, k_scales, v_scales, conv_weight):
    tok_rows = q_values.shape[0]
    head_count = q_scales.shape[1]
    seq_count = lax.axis_size(SEQ)
    marks_here = LANDMARKS // seq_count
    segment = tok_rows // marks_here
    query_rows = dequant(q_values, q_scales)
    key_rows = dequant(k_values, k_scales)
    value_rows = dequant(v_values, v_scales)

    def means(source):
        shaped = source.reshape(marks_here, segment, head_count, HEAD_DIM).astype(jnp.float32)
        return (
            jnp.mean(shaped, axis=1).astype(jnp.bfloat16).reshape(marks_here, head_count * HEAD_DIM)
        )

    query_landmarks, key_landmarks = side_by_side((means(query_rows), means(key_rows)), SEQ, 0, 1)
    query_landmarks = query_landmarks.reshape(LANDMARKS, head_count, HEAD_DIM)
    key_landmarks = key_landmarks.reshape(LANDMARKS, head_count, HEAD_DIM)
    pseudo_inverse_factor = HEAD_DIM ** (-0.5)
    landmark_kernel = (
        jnp.einsum(
            "jvc,kvc->vjk", query_landmarks, key_landmarks, preferred_element_type=jnp.float32
        )
        * pseudo_inverse_factor
    )
    middle = jax.nn.softmax(landmark_kernel, axis=-1)
    col_top = jnp.max(jnp.sum(middle, axis=1))
    row_top = jnp.max(jnp.sum(middle, axis=2))
    col_top, row_top = packed_total((col_top, row_top), "head")
    start = jnp.swapaxes(middle, 1, 2) / (col_top * row_top)
    distant_term = (
        jnp.einsum("kli,nli->lkn", query_landmarks, key_rows, preferred_element_type=jnp.float32)
        * pseudo_inverse_factor
    )
    far_top = by_axis(jnp.max(distant_term, axis=-1), SEQ)
    weight_matrix = jnp.exp(distant_term - far_top[:, :, None])
    total = jnp.sum(weight_matrix, axis=-1)
    summed = jnp.einsum(
        "lnx,xlj->nlj",
        weight_matrix.astype(jnp.bfloat16),
        value_rows,
        preferred_element_type=jnp.float32,
    )
    total, summed = (
        lax.psum(total.astype(jnp.bfloat16), SEQ).astype(jnp.float32),
        lax.psum(summed.astype(jnp.bfloat16), SEQ).astype(jnp.float32),
    )
    reduced = summed / jnp.swapaxes(total, 0, 1)[:, :, None]
    projected_values = jax.vmap(newton, in_axes=(0, 0, 1), out_axes=1)(middle, start, reduced)
    near_scores = (
        jnp.einsum("zea,uea->ezu", query_rows, key_landmarks, preferred_element_type=jnp.float32)
        * pseudo_inverse_factor
    )
    local_term = jax.nn.softmax(near_scores, axis=-1).astype(jnp.bfloat16)
    attended = jnp.einsum(
        "kbv,vkg->bkg", local_term, projected_values, preferred_element_type=jnp.float32
    ).reshape(tok_rows, head_count * HEAD_DIM)
    flat_values = value_rows.reshape(tok_rows, head_count * HEAD_DIM)
    tap_count = conv_weight.shape[1]
    padded = padded_2(flat_values, ((SEQ, 0),), tap_count // 2)
    tap_table = jnp.repeat(conv_weight, HEAD_DIM, axis=0)
    mixed = jnp.zeros((tok_rows, head_count * HEAD_DIM), jnp.float32)
    for tap_index in range(tap_count):
        mixed = (
            mixed
            + padded[tap_index : tap_index + tok_rows].astype(jnp.float32) * tap_table[:, tap_index]
        )
    return (attended + mixed).astype(jnp.bfloat16)


def solution(mesh):
    finer = Mesh(
        mesh.devices.reshape(4, 4, 2, mesh.shape["head"]), ("seq_0", "seq_1", "seq_2", "head")
    )
    placed = (
        P(SEQ, "head"),
        P(SEQ, "head"),
        P(SEQ, "head"),
        P(SEQ, "head"),
        P(SEQ, "head"),
        P(SEQ, "head"),
        P("head", None),
    )
    return jax.shard_map(
        shards, mesh=finer, in_specs=placed, out_specs=P(SEQ, "head"), check_vma=False
    )
```

profile of v0, /device:TPU:32, one launch (start us, length us, event | category | flops | bytes accessed | tf_op | source)
XLA Modules:
  0.0 302.6 jit_solution(4559212239840184039)
XLA Ops:
  6.5 4.7 %reshape.126 = f32[8,256,4,128]{3,2,1,0:T(4,128)} reshape(bf16[2048,512]{1,0:T(8,128)(2,1)} %param.7) | data formatting | bytes 6291456 | tf_op jit(solution)/shard_map/convert_element_type | solution.py:61
  11.7 4.6 %convert_reduce_fusion.1 = f32[8,4,128]{2,1,0:T(4,128)S(1)} fusion(f32[8,256,4,128]{3,2,1,0:T(4,128)} %reshape.126, f32[8,256,4]{2,1,0:T(8,128)S(1)} %bitcast.119), kind=kLoop, calls=%fused_computation.52 | loop fusion | flops 4190208 | bytes 4243456 | tf_op jit(solution)/shard_map/reduce_sum | solution.py:90
  16.3 3.0 reshape.127
  19.6 4.4 %convert_reduce_fusion = f32[8,4,128]{2,1,0:T(4,128)S(1)} fusion(f32[8,256,4,128]{3,2,1,0:T(4,128)} %reshape.127, f32[8,256,4]{2,1,0:T(8,128)S(1)} %bitcast.120), kind=kLoop, calls=%fused_computation.50 | loop fusion | flops 4190208 | bytes 4243456 | tf_op jit(solution)/shard_map/reduce_sum | solution.py:90
  24.1 25.1 %all_gather.3 = bf16[256,1024]{1,0:T(8,128)(2,1)S(1)} all-gather(bf16[8,1024]{1,0:T(8,128)(2,1)S(1)} %pad_maximum_fusion.2), channel_id=1, replica_groups=mesh['seq_0'=4,'seq_1'=4,'seq_2'=2,'head'=8] {'seq_0','seq_1','seq_2'}, dimensions={0}, use_global_device_ids=true | all-gather | bytes 540672 | tf_op jit(solution)/shard_map/all_gather | solution.py:16
  55.7 8.6 %all-to-all-start = ((f32[8,1,2]{2,1,0:T(1,128)}), f32[8,1,2]{2,1,0:T(1,128)S(1)}, u32[]{:S(2)}, u32[]{:S(2)}) async-start(f32[8,1,2]{2,1,0:T(1,128)} %broadcast_in_dim.4), calls=%async_computation | async-start | bytes 8192 | tf_op jit(solution)/shard_map/all_to_all | solution.py:25
  64.3 4.4 %multiply_reduce_fusion = (f32[4,256]{1,0:T(4,128)S(1)}, f32[4,256,2048]{2,1,0:T(8,128)}) fusion(bf16[256,4,128]{0,2,1:T(8,128)(2,1)S(1)} %bitcast.123, f32[2048,4]{0,1:T(4,128)S(1)} %copy-done.11, bf16[2048,512]{1,0:T(8,128)(2,1)S(1)} %copy-done.4), kind=kOutput, calls=%fused_computation.34 | convolution fusion | flops 544209920 | bytes 10784768 | tf_op jit(solution)/shard_map/kli,nli->lkn/dot_general | solution.py:109
  68.7 10.2 %pmax.21 = f32[4,256]{1,0:T(4,128)S(1)} all-reduce(f32[4,256]{1,0:T(4,128)S(1)} %get-tuple-element.48), channel_id=1, replica_groups=mesh['seq_0'=4,'seq_1'=4,'seq_2'=2,'head'=8] {'seq_0'}, use_global_device_ids=true, to_apply=%region_10.0 | all-reduce | flops 1024 | bytes 8192 | tf_op jit(solution)/shard_map/pmax | solution.py:43
  78.9 8.5 %pmax.22 = f32[4,256]{1,0:T(4,128)S(1)} all-reduce(f32[4,256]{1,0:T(4,128)S(1)} %pmax.21), channel_id=1, replica_groups=mesh['seq_0'=4,'seq_1'=4,'seq_2'=2,'head'=8] {'seq_1'}, use_global_device_ids=true, to_apply=%region_11.0 | all-reduce | flops 1024 | bytes 8192 | tf_op jit(solution)/shard_map/pmax | solution.py:43
  90.0 4.1 %copy.106 = f32[2048,512]{0,1:T(8,128)} copy(bf16[2048,512]{1,0:T(8,128)(2,1)} %param.9) | data formatting | bytes 6291456 | tf_op jit(solution)/shard_map/convert_element_type | solution.py:61
  94.1 2.7 multiply_convert_fusion.1
  96.8 5.9 %fusion.121 = bf16[256,4,128]{0,2,1:T(8,128)(2,1)} fusion(bf16[2048,4,128]{0,2,1:T(8,128)(2,1)S(1)} %multiply_convert_fusion.1, f32[4,256,2048]{2,1,0:T(8,128)} %get-tuple-element.49, f32[4,256]{1,0:T(4,128)S(1)} %pmax.23), kind=kOutput, calls=%fused_computation.148 | convolution fusion | flops 543293440 | bytes 10752000 | tf_op jit(solution)/shard_map/lnx,xlj->nlj/dot_general | solution.py:115
  106.6 4.4 %fusion.2 = bf16[4,256]{1,0:T(4,128)(2,1)S(1)} fusion(f32[4,256,2048]{2,1,0:T(8,128)} %get-tuple-element.49, f32[4,256]{1,0:T(4,128)S(1)} %pmax.23), kind=kLoop, calls=%fused_computation.37 | loop fusion | flops 6290432 | bytes 8394752 | tf_op jit(solution)/shard_map/reduce_sum | solution.py:114
  111.1 4.2 %fusion.16 = f32[4,2048,256]{1,2,0:T(8,128)} fusion(bf16[256,4,128]{0,2,1:T(8,128)(2,1)S(1)} %bitcast.125, f32[2048,4]{0,1:T(4,128)S(1)} %copy-done.12, bf16[2048,512]{1,0:T(8,128)(2,1)S(1)} %copy-done.5), kind=kOutput, calls=%fused_computation.56 | convolution fusion | flops 540016640 | bytes 10780672 | tf_op jit(solution)/shard_map/zea,uea->ezu/dot_general | solution.py:128
  116.9 11.7 %fusion.170 = (f32[4,2048]{1,0:T(4,128)S(1)}, f32[4,2048,256]{1,2,0:T(8,128)}) fusion(f32[4,2048,256]{1,2,0:T(8,128)} %fusion.16), kind=kOutput, calls=%fused_computation.199 | output fusion | flops 8388863 | bytes 16809984 | tf_op jit(solution)/shard_map/sub | solution.py:131
  128.6 2.5 mul.490
  131.1 5.3 %copy.108 = f32[2048,512]{1,0:T(8,128)} copy(f32[2048,512]{0,1:T(8,128)} %bitcast.118) | data formatting | bytes 8388608 | tf_op jit(solution)/shard_map/mul | solution.py:62
  136.5 4.9 %multiply_convert_fusion = bf16[2048,512]{1,0:T(8,128)(2,1)} fusion(f32[2048,512]{1,0:T(8,128)} %copy.108, bf16[2048,512]{1,0:T(8,128)(2,1)} %param.9), kind=kLoop, calls=%fused_computation.45 | loop fusion | flops 3145728 | bytes 8388608 | tf_op jit(solution)/shard_map/convert_element_type | solution.py:62
  141.4 64.7 %psum.15 = bf16[256,4]{0,1:T(4,128)(2,1)S(1)} all-reduce(bf16[256,4]{0,1:T(4,128)(2,1)S(1)} %bitcast.164), channel_id=1, replica_groups=mesh['seq_0'=4,'seq_1'=4,'seq_2'=2,'head'=8] {'seq_0','seq_1','seq_2'}, use_global_device_ids=true, to_apply=%region_15.0 | all-reduce | flops 1024 | bytes 4096 | tf_op jit(solution)/shard_map/psum | solution.py:122
  211.8 4.3 %online-softmax = f32[4,256,256]{2,1,0:T(8,128)} custom-call(f32[4,256,256]{2,1,0:T(8,128)} %copy-done, f32[4,256,256]{2,1,0:T(8,128)} %convolution_multiply_fusion.5), custom_call_target="tpu_custom_call" | custom-call | tf_op online-softmax
  216.2 2.6 fusion.77
  220.2 4.3 %online-softmax.1 = f32[4,256,256]{2,1,0:T(8,128)} custom-call(f32[4,256,256]{2,1,0:T(8,128)} %copy-done, f32[4,256,256]{2,1,0:T(8,128)} %convolution_multiply_fusion.4), custom_call_target="tpu_custom_call" | custom-call | tf_op online-softmax
  224.5 2.6 fusion.86
  228.5 4.3 %online-softmax.2 = f32[4,256,256]{2,1,0:T(8,128)} custom-call(f32[4,256,256]{2,1,0:T(8,128)} %copy-done, f32[4,256,256]{2,1,0:T(8,128)} %convolution_multiply_fusion.3), custom_call_target="tpu_custom_call" | custom-call | tf_op online-softmax
  232.8 2.6 fusion.95
  236.8 4.3 %online-softmax.3 = f32[4,256,256]{2,1,0:T(8,128)} custom-call(f32[4,256,256]{2,1,0:T(8,128)} %copy-done, f32[4,256,256]{2,1,0:T(8,128)} %convolution_multiply_fusion.2), custom_call_target="tpu_custom_call" | custom-call | tf_op online-softmax
  241.1 2.6 fusion.104
  245.1 4.3 %online-softmax.4 = f32[4,256,256]{2,1,0:T(8,128)} custom-call(f32[4,256,256]{2,1,0:T(8,128)} %copy-done, f32[4,256,256]{2,1,0:T(8,128)} %convolution_multiply_fusion.1), custom_call_target="tpu_custom_call" | custom-call | tf_op online-softmax
  249.5 2.6 fusion.113
  253.5 6.3 %fusion.13 = f32[4,128,2048]{2,1,0:T(8,128)} fusion(bf16[256,4,128]{2,0,1:T(8,128)(2,1)S(1)} %fusion.124, f32[4,2048,256]{1,2,0:T(8,128)} %get-tuple-element.51, f32[4,2048]{1,0:T(4,128)S(1)} %get-tuple-element.50), kind=kOutput, calls=%fused_computation.54 | convolution fusion | flops 541065216 | bytes 12877824 | tf_op jit(solution)/shard_map/kbv,vkg->bkg/dot_general | solution.py:132
  260.0 5.5 %copy.94 = f32[2048,512]{1,0:T(8,128)} copy(f32[2048,512]{0,1:T(8,128)} %bitcast.121) | data formatting | bytes 8388608 | tf_op jit(solution)/shard_map/reshape | solution.py:134
  265.9 29.8 %add_convert_fusion = bf16[2048,512]{1,0:T(8,128)(2,1)} fusion(f32[2048,512]{1,0:T(8,128)} %copy.94, bf16[2048,512]{1,0:T(8,128)(2,1)S(1)} %copy-done.6, bf16[16,512]{1,0:T(8,128)(2,1)S(1)} %collective-permute-done.1, bf16[16,512]{1,0:T(8,128)(2,1)S(1)} %collective-permute-done, f32[512]{0:T(512)S(1)} %bitcast.132, f32[512]{0:T(512)S(1)} %bitcast.133, ...), kind=kLoop, calls=%fused_computation.44 | loop fusion | flops 205520896 | bytes 8488960 | tf_op jit(solution)/shard_map/convert_element_type | solution.py:145
  (140 shorter events, 26.7 us)
Async XLA Ops:
  51.6 158.4 %copy-start = (f32[4,256,256]{2,1,0:T(8,128)}, f32[4,256,256]{2,1,0:T(8,128)S(1)}, u32[]{:S(2)}) copy-start(f32[4,256,256]{2,1,0:T(8,128)S(1)} %get-tuple-element.47) | copy-start | bytes 3145732
  55.7 150.4 %all-to-all-start = ((f32[8,1,2]{2,1,0:T(1,128)}), f32[8,1,2]{2,1,0:T(1,128)S(1)}, u32[]{:S(2)}, u32[]{:S(2)}) async-start(f32[8,1,2]{2,1,0:T(1,128)} %broadcast_in_dim.4), calls=%async_computation | async-start | bytes 8192 | tf_op jit(solution)/shard_map/all_to_all | solution.py:25
  64.3 187.8 %all-reduce.2.cloned.1.call-start = ((), (), s32[]{:S(2)}) async-start(), calls=%async_computation.1 | async-start | bytes 524288 | tf_op jit(solution)/shard_map/psum | solution.py:123
  68.7 25.4 %copy-start.10 = (f32[2048,4]{0,1:T(4,128)S(1)}, f32[2048,4]{0,1:T(4,128)}, u32[]{:S(2)}) copy-start(f32[2048,4]{0,1:T(4,128)} %param.12) | copy-start | bytes 98308
  102.9 162.7 %collective-permute-start = (bf16[16,512]{1,0:T(8,128)(2,1)S(1)}, bf16[16,512]{1,0:T(8,128)(2,1)S(1)}, u32[]{:S(2)}, u32[]{:S(2)}) collective-permute-start(bf16[16,512]{1,0:T(8,128)(2,1)S(1)} %copy.107), channel_id=1, source_target_pairs={{0,8},{8,16},{16,24},{24,32},{32,40},{40,48},{48,56},{56,64},{64,7... | collective-permute-start | bytes 49160 | tf_op jit(solution)/shard_map/ppermute | solution.py:53
  105.1 160.5 %collective-permute-start.1 = (bf16[16,512]{1,0:T(8,128)(2,1)S(1)}, bf16[16,512]{1,0:T(8,128)(2,1)S(1)}, u32[]{:S(2)}, u32[]{:S(2)}) collective-permute-start(bf16[16,512]{1,0:T(8,128)(2,1)S(1)} %copy.109), channel_id=1, source_target_pairs={{8,0},{16,8},{24,16},{32,24},{40,32},{48,40},{56,48},{64,56},{72,6... | collective-permute-start | bytes 49160 | tf_op jit(solution)/shard_map/ppermute | solution.py:54
  211.8 6.9 %copy-start.8 = (f32[4,256,256]{2,1,0:T(8,128)S(1)}, f32[4,256,256]{2,1,0:T(8,128)}, u32[]{:S(2)}) copy-start(f32[4,256,256]{2,1,0:T(8,128)} %convolution_multiply_fusion.5) | copy-start | bytes 3145732
  220.2 6.9 %copy-start.1 = (f32[4,256,256]{2,1,0:T(8,128)S(1)}, f32[4,256,256]{2,1,0:T(8,128)}, u32[]{:S(2)}) copy-start(f32[4,256,256]{2,1,0:T(8,128)} %convolution_multiply_fusion.4) | copy-start | bytes 3145732
  228.5 6.9 %copy-start.2 = (f32[4,256,256]{2,1,0:T(8,128)S(1)}, f32[4,256,256]{2,1,0:T(8,128)}, u32[]{:S(2)}) copy-start(f32[4,256,256]{2,1,0:T(8,128)} %convolution_multiply_fusion.3) | copy-start | bytes 3145732
  236.8 6.9 %copy-start.3 = (f32[4,256,256]{2,1,0:T(8,128)S(1)}, f32[4,256,256]{2,1,0:T(8,128)}, u32[]{:S(2)}) copy-start(f32[4,256,256]{2,1,0:T(8,128)} %convolution_multiply_fusion.2) | copy-start | bytes 3145732
  245.1 7.0 %copy-start.7 = (f32[4,256,256]{2,1,0:T(8,128)S(1)}, f32[4,256,256]{2,1,0:T(8,128)}, u32[]{:S(2)}) copy-start(f32[4,256,256]{2,1,0:T(8,128)} %convolution_multiply_fusion.1) | copy-start | bytes 3145732
  259.8 5.9 %copy-start.16 = (f32[512,1]{0,1:T(1,128)S(1)}, f32[512,1]{0,1:T(1,128)}, u32[]{:S(2)}) copy-start(f32[512,1]{0,1:T(1,128)} %get-tuple-element.15) | copy-start | bytes 6148
  259.8 5.9 %copy-start.17 = (f32[512,1]{0,1:T(1,128)S(1)}, f32[512,1]{0,1:T(1,128)}, u32[]{:S(2)}) copy-start(f32[512,1]{0,1:T(1,128)} %get-tuple-element.16) | copy-start | bytes 6148
  259.8 5.9 %copy-start.18 = (f32[512,1]{0,1:T(1,128)S(1)}, f32[512,1]{0,1:T(1,128)}, u32[]{:S(2)}) copy-start(f32[512,1]{0,1:T(1,128)} %get-tuple-element.17) | copy-start | bytes 6148
  259.8 5.9 %copy-start.19 = (f32[512,1]{0,1:T(1,128)S(1)}, f32[512,1]{0,1:T(1,128)}, u32[]{:S(2)}) copy-start(f32[512,1]{0,1:T(1,128)} %get-tuple-element.18) | copy-start | bytes 6148
  259.8 5.9 %copy-start.20 = (f32[512,1]{0,1:T(1,128)S(1)}, f32[512,1]{0,1:T(1,128)}, u32[]{:S(2)}) copy-start(f32[512,1]{0,1:T(1,128)} %get-tuple-element.19) | copy-start | bytes 6148
  259.8 5.9 %copy-start.21 = (f32[512,1]{0,1:T(1,128)S(1)}, f32[512,1]{0,1:T(1,128)}, u32[]{:S(2)}) copy-start(f32[512,1]{0,1:T(1,128)} %get-tuple-element.20) | copy-start | bytes 6148
  259.8 5.9 %copy-start.22 = (f32[512,1]{0,1:T(1,128)S(1)}, f32[512,1]{0,1:T(1,128)}, u32[]{:S(2)}) copy-start(f32[512,1]{0,1:T(1,128)} %get-tuple-element.21) | copy-start | bytes 6148
  259.8 5.9 %copy-start.23 = (f32[512,1]{0,1:T(1,128)S(1)}, f32[512,1]{0,1:T(1,128)}, u32[]{:S(2)}) copy-start(f32[512,1]{0,1:T(1,128)} %get-tuple-element.22) | copy-start | bytes 6148
  259.8 5.9 %copy-start.24 = (f32[512,1]{0,1:T(1,128)S(1)}, f32[512,1]{0,1:T(1,128)}, u32[]{:S(2)}) copy-start(f32[512,1]{0,1:T(1,128)} %get-tuple-element.23) | copy-start | bytes 6148
  259.8 5.9 %copy-start.25 = (f32[512,1]{0,1:T(1,128)S(1)}, f32[512,1]{0,1:T(1,128)}, u32[]{:S(2)}) copy-start(f32[512,1]{0,1:T(1,128)} %get-tuple-element.24) | copy-start | bytes 6148
  259.9 5.9 %copy-start.26 = (f32[512,1]{0,1:T(1,128)S(1)}, f32[512,1]{0,1:T(1,128)}, u32[]{:S(2)}) copy-start(f32[512,1]{0,1:T(1,128)} %get-tuple-element.25) | copy-start | bytes 6148
  259.9 5.9 %copy-start.27 = (f32[512,1]{0,1:T(1,128)S(1)}, f32[512,1]{0,1:T(1,128)}, u32[]{:S(2)}) copy-start(f32[512,1]{0,1:T(1,128)} %get-tuple-element.26) | copy-start | bytes 6148
  259.9 5.9 %copy-start.28 = (f32[512,1]{0,1:T(1,128)S(1)}, f32[512,1]{0,1:T(1,128)}, u32[]{:S(2)}) copy-start(f32[512,1]{0,1:T(1,128)} %get-tuple-element.27) | copy-start | bytes 6148
  259.9 5.9 %copy-start.29 = (f32[512,1]{0,1:T(1,128)S(1)}, f32[512,1]{0,1:T(1,128)}, u32[]{:S(2)}) copy-start(f32[512,1]{0,1:T(1,128)} %get-tuple-element.28) | copy-start | bytes 6148
  259.9 5.9 %copy-start.30 = (f32[512,1]{0,1:T(1,128)S(1)}, f32[512,1]{0,1:T(1,128)}, u32[]{:S(2)}) copy-start(f32[512,1]{0,1:T(1,128)} %get-tuple-element.29) | copy-start | bytes 6148
  259.9 5.9 %copy-start.31 = (f32[512,1]{0,1:T(1,128)S(1)}, f32[512,1]{0,1:T(1,128)}, u32[]{:S(2)}) copy-start(f32[512,1]{0,1:T(1,128)} %get-tuple-element.30) | copy-start | bytes 6148
  259.9 5.9 %copy-start.32 = (f32[512,1]{0,1:T(1,128)S(1)}, f32[512,1]{0,1:T(1,128)}, u32[]{:S(2)}) copy-start(f32[512,1]{0,1:T(1,128)} %get-tuple-element.31) | copy-start | bytes 6148
  259.9 5.9 %copy-start.33 = (f32[512,1]{0,1:T(1,128)S(1)}, f32[512,1]{0,1:T(1,128)}, u32[]{:S(2)}) copy-start(f32[512,1]{0,1:T(1,128)} %get-tuple-element.32) | copy-start | bytes 6148
  259.9 5.9 %copy-start.34 = (f32[512,1]{0,1:T(1,128)S(1)}, f32[512,1]{0,1:T(1,128)}, u32[]{:S(2)}) copy-start(f32[512,1]{0,1:T(1,128)} %get-tuple-element.33) | copy-start | bytes 6148
  259.9 5.9 %copy-start.35 = (f32[512,1]{0,1:T(1,128)S(1)}, f32[512,1]{0,1:T(1,128)}, u32[]{:S(2)}) copy-start(f32[512,1]{0,1:T(1,128)} %get-tuple-element.34) | copy-start | bytes 6148
  259.9 5.9 %copy-start.36 = (f32[512,1]{0,1:T(1,128)S(1)}, f32[512,1]{0,1:T(1,128)}, u32[]{:S(2)}) copy-start(f32[512,1]{0,1:T(1,128)} %get-tuple-element.35) | copy-start | bytes 6148
  (18 other events, 96.1 us)
Sparse Core Ops, SparseCore 0:
  102.8 108.5 all-reduce.1
where the time goes:
time: 304 us; the launch traced here: 303 us
  blocking collectives  111 us (37%)
  other arithmetic  66.2 us (22%)
  matrix products  45.7 us (15%)
  local copies, waits for them, and re-layouts  30.2 us (10%)
  Pallas kernels  21.7 us (7%)
  between operations  15.5 us (5%)
  starting transfers between devices  12.1 us (4%)
    psum x1, blocking collectives, shards(): lax.psum(total.astype(jnp.bfloat16), SEQ).astype(jnp.float32)  64.7 us
    convert_element_type x1, other arithmetic, shards(): return (attended + mixed).astype(jnp.bfloat16)  29.8 us
    all_gather x1, blocking collectives, side_by_side(): lax.all_gather(both, axis, axis=dim, tiled=True)  25.1 us
    unnamed x5, Pallas kernels  21.7 us
    pmax x3, blocking collectives, by_axis(): return functools.reduce(lax.pmax, axes, shard)  21.3 us
    dot_general x6, matrix products, newton(): inner_term = 13.0 * eye_matrix - jnp.dot(product, inner_term)  13.4 us
    convert_element_type x3, local copies, waits for them, and re-layouts, dequant(): value_rows.reshape(value_rows.shape[0], count, HEAD_DIM).astype(jnp.float32)  11.9 us
    sub x1, other arithmetic, shards(): local_term = jax.nn.softmax(near_scores, axis=-1).astype(jnp.bfloat16)  11.7 us
  transfers between devices with their start and end apart: 4, of which 0 were waited for; matrix products, arithmetic and copies ran while one was open for 29% of the time, Pallas kernels for 7%

commit v1 on v0

--- a/solution.py
+++ b/solution.py
@@ -119,7 +119,7 @@
         preferred_element_type=jnp.float32,
     )
     total, summed = (
-        lax.psum(total.astype(jnp.bfloat16), SEQ).astype(jnp.float32),
+        jnp.sum(lax.all_gather(total.astype(jnp.bfloat16), SEQ), axis=0).astype(jnp.float32),
         lax.psum(summed.astype(jnp.bfloat16), SEQ).astype(jnp.float32),
     )
     reduced = summed / jnp.swapaxes(total, 0, 1)[:, :, None]

time: 304 us -> 267 us (0.88)
  blocking collectives: 111 us -> 73.2 us
    psum x1 -> x0, blocking collectives: 64.7 us -> none  [shards(): lax.psum(total.astype(jnp.bfloat16), SEQ).astype(jnp.float32)]
    all_gather x0 -> x1, blocking collectives: none -> 26.8 us  [shards(): lax.all_gather(total.astype(jnp.bfloat16), SEQ)]
  transfers between devices with their start and end apart: 4 -> 4, of which waited for: 0 -> 0; matrix products, arithmetic and copies ran while one was open for 29% -> 33% of each run, Pallas kernels for 7% -> 8%
where the time goes in v1:
time: 267 us; the launch traced here: 265 us
  blocking collectives  73.2 us (27%)
  other arithmetic  66.8 us (25%)
  matrix products  45.7 us (17%)
  local copies, waits for them, and re-layouts  30.2 us (11%)
  Pallas kernels  21.6 us (8%)
  between operations  15.4 us (6%)
  starting transfers between devices  11.9 us (4%)
    convert_element_type x1, other arithmetic, shards(): return (attended + mixed).astype(jnp.bfloat16)  29.8 us
    all_gather x1, blocking collectives, shards(): lax.all_gather(total.astype(jnp.bfloat16), SEQ)  26.8 us
    all_gather x1, blocking collectives, side_by_side(): lax.all_gather(both, axis, axis=dim, tiled=True)  25.1 us
    unnamed x5, Pallas kernels  21.6 us
    pmax x3, blocking collectives, by_axis(): return functools.reduce(lax.pmax, axes, shard)  21.3 us
    dot_general x6, matrix products, newton(): inner_term = 13.0 * eye_matrix - jnp.dot(product, inner_term)  13.5 us
    convert_element_type x3, local copies, waits for them, and re-layouts, dequant(): value_rows.reshape(value_rows.shape[0], count, HEAD_DIM).astype(jnp.float32)  11.9 us
    sub x1, other arithmetic, shards(): local_term = jax.nn.softmax(near_scores, axis=-1).astype(jnp.bfloat16)  11.7 us
  transfers between devices with their start and end apart: 4, of which 0 were waited for; matrix products, arithmetic and copies ran while one was open for 33% of the time, Pallas kernels for 8%

profile of v1, /device:TPU:32, one launch (start us, length us, event | category | flops | bytes accessed | tf_op | source)
XLA Modules:
  0.0 264.9 jit_solution(17511866037577358979)
XLA Ops:
  6.5 4.8 %reshape.134 = f32[8,256,4,128]{3,2,1,0:T(4,128)} reshape(bf16[2048,512]{1,0:T(8,128)(2,1)} %param.7) | data formatting | bytes 6291456 | tf_op jit(solution)/shard_map/convert_element_type | solution.py:61
  11.7 4.6 %convert_reduce_fusion.1 = f32[8,4,128]{2,1,0:T(4,128)S(1)} fusion(f32[8,256,4,128]{3,2,1,0:T(4,128)} %reshape.134, f32[8,256,4]{2,1,0:T(8,128)S(1)} %bitcast.121), kind=kLoop, calls=%fused_computation.52 | loop fusion | flops 4190208 | bytes 4243456 | tf_op jit(solution)/shard_map/reduce_sum | solution.py:90
  16.3 3.0 %reshape.135 = f32[8,256,4,128]{3,2,1,0:T(4,128)} reshape(bf16[2048,512]{1,0:T(8,128)(2,1)S(1)} %copy-done.4) | data formatting | bytes 6291456 | tf_op jit(solution)/shard_map/convert_element_type | solution.py:61
  19.6 4.4 %convert_reduce_fusion = f32[8,4,128]{2,1,0:T(4,128)S(1)} fusion(f32[8,256,4,128]{3,2,1,0:T(4,128)} %reshape.135, f32[8,256,4]{2,1,0:T(8,128)S(1)} %bitcast.122), kind=kLoop, calls=%fused_computation.50 | loop fusion | flops 4190208 | bytes 4243456 | tf_op jit(solution)/shard_map/reduce_sum | solution.py:90
  24.1 25.1 %all_gather.7 = bf16[256,1024]{1,0:T(8,128)(2,1)S(1)} all-gather(bf16[8,1024]{1,0:T(8,128)(2,1)S(1)} %pad_maximum_fusion.2), channel_id=1, replica_groups=mesh['seq_0'=4,'seq_1'=4,'seq_2'=2,'head'=8] {'seq_0','seq_1','seq_2'}, dimensions={0}, use_global_device_ids=true | all-gather | bytes 540672 | tf_op jit(solution)/shard_map/all_gather | solution.py:16
  55.7 8.6 %all-to-all-start = ((f32[8,1,2]{2,1,0:T(1,128)}), f32[8,1,2]{2,1,0:T(1,128)S(1)}, u32[]{:S(2)}, u32[]{:S(2)}) async-start(f32[8,1,2]{2,1,0:T(1,128)} %broadcast_in_dim.4), calls=%async_computation | async-start | bytes 8192 | tf_op jit(solution)/shard_map/all_to_all | solution.py:25
  64.3 4.4 %multiply_reduce_fusion = (f32[4,256]{1,0:T(4,128)S(1)}, f32[4,256,2048]{2,1,0:T(8,128)}) fusion(bf16[256,4,128]{0,2,1:T(8,128)(2,1)S(1)} %bitcast.125, f32[2048,4]{0,1:T(4,128)S(1)} %copy-done.11, bf16[2048,512]{1,0:T(8,128)(2,1)S(1)} %copy-done.4), kind=kOutput, calls=%fused_computation.34 | convolution fusion | flops 544209920 | bytes 10784768 | tf_op jit(solution)/shard_map/kli,nli->lkn/dot_general | solution.py:109
  68.7 10.2 %pmax.21 = f32[4,256]{1,0:T(4,128)S(1)} all-reduce(f32[4,256]{1,0:T(4,128)S(1)} %get-tuple-element.48), channel_id=1, replica_groups=mesh['seq_0'=4,'seq_1'=4,'seq_2'=2,'head'=8] {'seq_0'}, use_global_device_ids=true, to_apply=%region_10.0 | all-reduce | flops 1024 | bytes 8192 | tf_op jit(solution)/shard_map/pmax | solution.py:43
  78.9 8.6 %pmax.22 = f32[4,256]{1,0:T(4,128)S(1)} all-reduce(f32[4,256]{1,0:T(4,128)S(1)} %pmax.21), channel_id=1, replica_groups=mesh['seq_0'=4,'seq_1'=4,'seq_2'=2,'head'=8] {'seq_1'}, use_global_device_ids=true, to_apply=%region_11.0 | all-reduce | flops 1024 | bytes 8192 | tf_op jit(solution)/shard_map/pmax | solution.py:43
  89.9 4.2 %copy.106 = f32[2048,512]{0,1:T(8,128)} copy(bf16[2048,512]{1,0:T(8,128)(2,1)} %param.9) | data formatting | bytes 6291456 | tf_op jit(solution)/shard_map/convert_element_type | solution.py:61
  94.1 2.7 %multiply_convert_fusion.1 = bf16[2048,4,128]{0,2,1:T(8,128)(2,1)S(1)} fusion(f32[2048,4,128]{0,2,1:T(8,128)} %bitcast.119, f32[2048,4]{0,1:T(4,128)S(1)} %copy-done.10), kind=kLoop, calls=%fused_computation.49 | loop fusion | flops 2097152 | bytes 6324224 | tf_op jit(solution)/shard_map/convert_element_type | solution.py:62
  96.8 5.9 %fusion.121 = bf16[256,4,128]{0,2,1:T(8,128)(2,1)} fusion(bf16[2048,4,128]{0,2,1:T(8,128)(2,1)S(1)} %multiply_convert_fusion.1, f32[4,256,2048]{2,1,0:T(8,128)} %get-tuple-element.49, f32[4,256]{1,0:T(4,128)S(1)} %pmax.23), kind=kOutput, calls=%fused_computation.148 | convolution fusion | flops 543293440 | bytes 10752000 | tf_op jit(solution)/shard_map/lnx,xlj->nlj/dot_general | solution.py:115
  106.4 4.4 %fusion.2 = bf16[4,256]{1,0:T(4,128)(2,1)S(1)} fusion(f32[4,256,2048]{2,1,0:T(8,128)} %get-tuple-element.49, f32[4,256]{1,0:T(4,128)S(1)} %pmax.23), kind=kLoop, calls=%fused_computation.37 | loop fusion | flops 6290432 | bytes 8394752 | tf_op jit(solution)/shard_map/reduce_sum | solution.py:114
  110.9 4.2 %fusion.16 = f32[4,2048,256]{1,2,0:T(8,128)} fusion(bf16[256,4,128]{0,2,1:T(8,128)(2,1)S(1)} %bitcast.127, f32[2048,4]{0,1:T(4,128)S(1)} %copy-done.12, bf16[2048,512]{1,0:T(8,128)(2,1)S(1)} %copy-done.5), kind=kOutput, calls=%fused_computation.56 | convolution fusion | flops 540016640 | bytes 10780672 | tf_op jit(solution)/shard_map/zea,uea->ezu/dot_general | solution.py:128
  116.7 26.8 %all-gather.1 = bf16[32,4,256]{2,1,0:T(4,128)(2,1)S(1)} all-gather(bf16[1,4,256]{2,1,0:T(4,128)(2,1)S(1)} %bitcast.166), channel_id=2, replica_groups=mesh['seq_0'=4,'seq_1'=4,'seq_2'=2,'head'=8] {'seq_0','seq_1','seq_2'}, dimensions={0}, use_global_device_ids=true | all-gather | bytes 67584 | tf_op jit(solution)/shard_map/all_gather | solution.py:122
  144.2 11.7 %fusion.170 = (f32[4,2048]{1,0:T(4,128)S(1)}, f32[4,2048,256]{1,2,0:T(8,128)}) fusion(f32[4,2048,256]{1,2,0:T(8,128)} %fusion.16), kind=kOutput, calls=%fused_computation.200 | output fusion | flops 8388863 | bytes 16809984 | tf_op jit(solution)/shard_map/sub | solution.py:131
  155.9 2.5 mul.490
  158.4 5.3 %copy.108 = f32[2048,512]{1,0:T(8,128)} copy(f32[2048,512]{0,1:T(8,128)} %bitcast.120) | data formatting | bytes 8388608 | tf_op jit(solution)/shard_map/mul | solution.py:62
  163.7 4.9 %multiply_convert_fusion = bf16[2048,512]{1,0:T(8,128)(2,1)} fusion(f32[2048,512]{1,0:T(8,128)} %copy.108, bf16[2048,512]{1,0:T(8,128)(2,1)} %param.9), kind=kLoop, calls=%fused_computation.45 | loop fusion | flops 3145728 | bytes 8388608 | tf_op jit(solution)/shard_map/convert_element_type | solution.py:62
  174.2 4.3 %online-softmax = f32[4,256,256]{2,1,0:T(8,128)} custom-call(f32[4,256,256]{2,1,0:T(8,128)} %copy-done, f32[4,256,256]{2,1,0:T(8,128)} %convolution_multiply_fusion.5), custom_call_target="tpu_custom_call" | custom-call | tf_op online-softmax
  178.5 2.6 fusion.77
  182.5 4.3 %online-softmax.1 = f32[4,256,256]{2,1,0:T(8,128)} custom-call(f32[4,256,256]{2,1,0:T(8,128)} %copy-done, f32[4,256,256]{2,1,0:T(8,128)} %convolution_multiply_fusion.4), custom_call_target="tpu_custom_call" | custom-call | tf_op online-softmax
  186.8 2.6 fusion.86
  190.8 4.3 %online-softmax.2 = f32[4,256,256]{2,1,0:T(8,128)} custom-call(f32[4,256,256]{2,1,0:T(8,128)} %copy-done, f32[4,256,256]{2,1,0:T(8,128)} %convolution_multiply_fusion.3), custom_call_target="tpu_custom_call" | custom-call | tf_op online-softmax
  195.1 2.6 fusion.95
  199.1 4.3 %online-softmax.3 = f32[4,256,256]{2,1,0:T(8,128)} custom-call(f32[4,256,256]{2,1,0:T(8,128)} %copy-done, f32[4,256,256]{2,1,0:T(8,128)} %convolution_multiply_fusion.2), custom_call_target="tpu_custom_call" | custom-call | tf_op online-softmax
  203.4 2.6 fusion.104
  207.4 4.3 %online-softmax.4 = f32[4,256,256]{2,1,0:T(8,128)} custom-call(f32[4,256,256]{2,1,0:T(8,128)} %copy-done, f32[4,256,256]{2,1,0:T(8,128)} %convolution_multiply_fusion.1), custom_call_target="tpu_custom_call" | custom-call | tf_op online-softmax
  211.7 2.6 fusion.113
  215.8 6.2 %fusion.13 = f32[4,128,2048]{2,1,0:T(8,128)} fusion(bf16[256,4,128]{2,0,1:T(8,128)(2,1)S(1)} %fusion.124, f32[4,2048,256]{1,2,0:T(8,128)} %get-tuple-element.51, f32[4,2048]{1,0:T(4,128)S(1)} %get-tuple-element.50), kind=kOutput, calls=%fused_computation.54 | convolution fusion | flops 541065216 | bytes 12877824 | tf_op jit(solution)/shard_map/kbv,vkg->bkg/dot_general | solution.py:132
  222.3 5.5 %copy.94 = f32[2048,512]{1,0:T(8,128)} copy(f32[2048,512]{0,1:T(8,128)} %bitcast.123) | data formatting | bytes 8388608 | tf_op jit(solution)/shard_map/reshape | solution.py:134
  228.2 29.8 %add_convert_fusion = bf16[2048,512]{1,0:T(8,128)(2,1)} fusion(f32[2048,512]{1,0:T(8,128)} %copy.94, bf16[2048,512]{1,0:T(8,128)(2,1)S(1)} %copy-done.6, bf16[16,512]{1,0:T(8,128)(2,1)S(1)} %collective-permute-done.1, bf16[16,512]{1,0:T(8,128)(2,1)S(1)} %collective-permute-done, f32[512]{0:T(512)S(1)} %bitcast.134, f32[512]{0:T(512)S(1)} %bitcast.135, ...), kind=kLoop, calls=%fused_computation.44 | loop fusion | flops 205520896 | bytes 8488960 | tf_op jit(solution)/shard_map/convert_element_type | solution.py:145
  (143 shorter events, 27.0 us)
Async XLA Ops:
  51.6 120.8 %copy-start = (f32[4,256,256]{2,1,0:T(8,128)}, f32[4,256,256]{2,1,0:T(8,128)S(1)}, u32[]{:S(2)}) copy-start(f32[4,256,256]{2,1,0:T(8,128)S(1)} %get-tuple-element.47) | copy-start | bytes 3145732
  55.7 112.9 %all-to-all-start = ((f32[8,1,2]{2,1,0:T(1,128)}), f32[8,1,2]{2,1,0:T(1,128)S(1)}, u32[]{:S(2)}, u32[]{:S(2)}) async-start(f32[8,1,2]{2,1,0:T(1,128)} %broadcast_in_dim.4), calls=%async_computation | async-start | bytes 8192 | tf_op jit(solution)/shard_map/all_to_all | solution.py:25
  64.3 150.1 %all-reduce.2.cloned.1.call-start = ((), (), s32[]{:S(2)}) async-start(), calls=%async_computation.1 | async-start | bytes 524288 | tf_op jit(solution)/shard_map/psum | solution.py:123
  68.7 25.4 %copy-start.10 = (f32[2048,4]{0,1:T(4,128)S(1)}, f32[2048,4]{0,1:T(4,128)}, u32[]{:S(2)}) copy-start(f32[2048,4]{0,1:T(4,128)} %param.12) | copy-start | bytes 98308
  102.9 124.9 %collective-permute-start = (bf16[16,512]{1,0:T(8,128)(2,1)S(1)}, bf16[16,512]{1,0:T(8,128)(2,1)S(1)}, u32[]{:S(2)}, u32[]{:S(2)}) collective-permute-start(bf16[16,512]{1,0:T(8,128)(2,1)S(1)} %copy.107), channel_id=1, source_target_pairs={{0,8},{8,16},{16,24},{24,32},{32,40},{40,48},{48,56},{56,64},{64,7... | collective-permute-start | bytes 49160 | tf_op jit(solution)/shard_map/ppermute | solution.py:53
  105.1 122.8 %collective-permute-start.1 = (bf16[16,512]{1,0:T(8,128)(2,1)S(1)}, bf16[16,512]{1,0:T(8,128)(2,1)S(1)}, u32[]{:S(2)}, u32[]{:S(2)}) collective-permute-start(bf16[16,512]{1,0:T(8,128)(2,1)S(1)} %copy.109), channel_id=1, source_target_pairs={{8,0},{16,8},{24,16},{32,24},{40,32},{48,40},{56,48},{64,56},{72,6... | collective-permute-start | bytes 49160 | tf_op jit(solution)/shard_map/ppermute | solution.py:54
  174.2 6.9 %copy-start.8 = (f32[4,256,256]{2,1,0:T(8,128)S(1)}, f32[4,256,256]{2,1,0:T(8,128)}, u32[]{:S(2)}) copy-start(f32[4,256,256]{2,1,0:T(8,128)} %convolution_multiply_fusion.5) | copy-start | bytes 3145732
  182.5 6.9 %copy-start.1 = (f32[4,256,256]{2,1,0:T(8,128)S(1)}, f32[4,256,256]{2,1,0:T(8,128)}, u32[]{:S(2)}) copy-start(f32[4,256,256]{2,1,0:T(8,128)} %convolution_multiply_fusion.4) | copy-start | bytes 3145732
  190.8 6.9 %copy-start.2 = (f32[4,256,256]{2,1,0:T(8,128)S(1)}, f32[4,256,256]{2,1,0:T(8,128)}, u32[]{:S(2)}) copy-start(f32[4,256,256]{2,1,0:T(8,128)} %convolution_multiply_fusion.3) | copy-start | bytes 3145732
  199.1 6.9 %copy-start.3 = (f32[4,256,256]{2,1,0:T(8,128)S(1)}, f32[4,256,256]{2,1,0:T(8,128)}, u32[]{:S(2)}) copy-start(f32[4,256,256]{2,1,0:T(8,128)} %convolution_multiply_fusion.2) | copy-start | bytes 3145732
  207.4 6.9 %copy-start.7 = (f32[4,256,256]{2,1,0:T(8,128)S(1)}, f32[4,256,256]{2,1,0:T(8,128)}, u32[]{:S(2)}) copy-start(f32[4,256,256]{2,1,0:T(8,128)} %convolution_multiply_fusion.1) | copy-start | bytes 3145732
  207.4 7.0 %copy-start.45 = (f32[256,4]{0,1:T(4,128)S(1)}, f32[256,4]{0,1:T(4,128)}, u32[]{:S(2)}) copy-start(f32[256,4]{0,1:T(4,128)} %convert_bitcast_fusion.2) | copy-start | bytes 12292
  222.0 5.9 %copy-start.16 = (f32[512,1]{0,1:T(1,128)S(1)}, f32[512,1]{0,1:T(1,128)}, u32[]{:S(2)}) copy-start(f32[512,1]{0,1:T(1,128)} %get-tuple-element.15) | copy-start | bytes 6148
  222.0 5.9 %copy-start.17 = (f32[512,1]{0,1:T(1,128)S(1)}, f32[512,1]{0,1:T(1,128)}, u32[]{:S(2)}) copy-start(f32[512,1]{0,1:T(1,128)} %get-tuple-element.16) | copy-start | bytes 6148
  222.1 5.9 %copy-start.18 = (f32[512,1]{0,1:T(1,128)S(1)}, f32[512,1]{0,1:T(1,128)}, u32[]{:S(2)}) copy-start(f32[512,1]{0,1:T(1,128)} %get-tuple-element.17) | copy-start | bytes 6148
  222.1 5.9 %copy-start.19 = (f32[512,1]{0,1:T(1,128)S(1)}, f32[512,1]{0,1:T(1,128)}, u32[]{:S(2)}) copy-start(f32[512,1]{0,1:T(1,128)} %get-tuple-element.18) | copy-start | bytes 6148
  222.1 5.9 %copy-start.20 = (f32[512,1]{0,1:T(1,128)S(1)}, f32[512,1]{0,1:T(1,128)}, u32[]{:S(2)}) copy-start(f32[512,1]{0,1:T(1,128)} %get-tuple-element.19) | copy-start | bytes 6148
  222.1 5.9 %copy-start.21 = (f32[512,1]{0,1:T(1,128)S(1)}, f32[512,1]{0,1:T(1,128)}, u32[]{:S(2)}) copy-start(f32[512,1]{0,1:T(1,128)} %get-tuple-element.20) | copy-start | bytes 6148
  222.1 5.9 %copy-start.22 = (f32[512,1]{0,1:T(1,128)S(1)}, f32[512,1]{0,1:T(1,128)}, u32[]{:S(2)}) copy-start(f32[512,1]{0,1:T(1,128)} %get-tuple-element.21) | copy-start | bytes 6148
  222.1 5.9 %copy-start.23 = (f32[512,1]{0,1:T(1,128)S(1)}, f32[512,1]{0,1:T(1,128)}, u32[]{:S(2)}) copy-start(f32[512,1]{0,1:T(1,128)} %get-tuple-element.22) | copy-start | bytes 6148
  222.1 5.9 %copy-start.24 = (f32[512,1]{0,1:T(1,128)S(1)}, f32[512,1]{0,1:T(1,128)}, u32[]{:S(2)}) copy-start(f32[512,1]{0,1:T(1,128)} %get-tuple-element.23) | copy-start | bytes 6148
  222.1 5.9 %copy-start.25 = (f32[512,1]{0,1:T(1,128)S(1)}, f32[512,1]{0,1:T(1,128)}, u32[]{:S(2)}) copy-start(f32[512,1]{0,1:T(1,128)} %get-tuple-element.24) | copy-start | bytes 6148
  222.1 5.9 %copy-start.26 = (f32[512,1]{0,1:T(1,128)S(1)}, f32[512,1]{0,1:T(1,128)}, u32[]{:S(2)}) copy-start(f32[512,1]{0,1:T(1,128)} %get-tuple-element.25) | copy-start | bytes 6148
  222.1 5.9 %copy-start.27 = (f32[512,1]{0,1:T(1,128)S(1)}, f32[512,1]{0,1:T(1,128)}, u32[]{:S(2)}) copy-start(f32[512,1]{0,1:T(1,128)} %get-tuple-element.26) | copy-start | bytes 6148
  222.2 5.9 %copy-start.28 = (f32[512,1]{0,1:T(1,128)S(1)}, f32[512,1]{0,1:T(1,128)}, u32[]{:S(2)}) copy-start(f32[512,1]{0,1:T(1,128)} %get-tuple-element.27) | copy-start | bytes 6148
  222.2 5.9 %copy-start.29 = (f32[512,1]{0,1:T(1,128)S(1)}, f32[512,1]{0,1:T(1,128)}, u32[]{:S(2)}) copy-start(f32[512,1]{0,1:T(1,128)} %get-tuple-element.28) | copy-start | bytes 6148
  222.2 5.9 %copy-start.30 = (f32[512,1]{0,1:T(1,128)S(1)}, f32[512,1]{0,1:T(1,128)}, u32[]{:S(2)}) copy-start(f32[512,1]{0,1:T(1,128)} %get-tuple-element.29) | copy-start | bytes 6148
  222.2 5.9 %copy-start.31 = (f32[512,1]{0,1:T(1,128)S(1)}, f32[512,1]{0,1:T(1,128)}, u32[]{:S(2)}) copy-start(f32[512,1]{0,1:T(1,128)} %get-tuple-element.30) | copy-start | bytes 6148
  222.2 5.9 %copy-start.32 = (f32[512,1]{0,1:T(1,128)S(1)}, f32[512,1]{0,1:T(1,128)}, u32[]{:S(2)}) copy-start(f32[512,1]{0,1:T(1,128)} %get-tuple-element.31) | copy-start | bytes 6148
  222.2 5.9 %copy-start.33 = (f32[512,1]{0,1:T(1,128)S(1)}, f32[512,1]{0,1:T(1,128)}, u32[]{:S(2)}) copy-start(f32[512,1]{0,1:T(1,128)} %get-tuple-element.32) | copy-start | bytes 6148
  222.2 5.9 %copy-start.34 = (f32[512,1]{0,1:T(1,128)S(1)}, f32[512,1]{0,1:T(1,128)}, u32[]{:S(2)}) copy-start(f32[512,1]{0,1:T(1,128)} %get-tuple-element.33) | copy-start | bytes 6148
  222.2 5.9 %copy-start.35 = (f32[512,1]{0,1:T(1,128)S(1)}, f32[512,1]{0,1:T(1,128)}, u32[]{:S(2)}) copy-start(f32[512,1]{0,1:T(1,128)} %get-tuple-element.34) | copy-start | bytes 6148
  (19 other events, 102.1 us)
Sparse Core Ops, SparseCore 0:
  102.9 108.6 all-reduce.1
